TPU v7x, 256 devices: a whole 4x4x8 slice. The times are simulated.
256 devices in a mesh: seq: 64 (over x, z, core), grp: 4 (over y).
Axes of the slice: x: 4, y: 4, z: 8, core: 2. Of those that a mesh axis runs over, the one named last changes fastest.
Arguments:
- queries: bfloat16 [4, 8192, 640], P('grp', 'seq'), may hold values from -120 to 120
- comp_kv: bfloat16 [4, 8192, 256], P('grp', 'seq'), may hold values from -6 to 6
- out_grad: bfloat16 [4, 8192, 640], P('grp', 'seq'), may hold values from -6 to 6
- comp_ids: int32 [4, 8192], P('grp', 'seq'), may hold values from 0 to 7, as said below
- comp_pos: int32 [4, 8192], P('grp', 'seq'), may hold values from 0 to 4095, as said below
- prompt_kv: bfloat16 [4, 4096, 256], P('grp', 'seq'), may hold values from -6 to 6
- owned_prompt: int32 [4], replicated, may hold values from 0 to 3, each once
Outputs:
- grad_queries: bfloat16 [4, 8192, 640], P('grp', 'seq')
- grad_comp_kv: bfloat16 [4, 8192, 256], P('grp', 'seq')
- grad_prompt_kv: bfloat16 [4, 4096, 256], P('grp', 'seq')
Inputs may be any that keep to these rules, and one draw needn't show every extreme that they name: `comp_ids`: completions 0 to 7 each hold whole blocks of 32 consecutive positions; each is packed in blocks of 32 tokens in an arbitrary order over the token axis; the longest completion has exactly 128 blocks. `comp_pos`: the tokens of one completion hold positions 0 to its length minus one, each once.
All inputs are finite; a program needn't handle non-finite values.
Results may differ from a plain program's by a relative error of at most 0.005.
Values may be sent and summed in bfloat16 or wider, within the bound.
A program may use at most 128 MiB of HBM per device.

v0:
```python
import math

import jax
import jax.numpy as jnp
from jax import lax
from jax.experimental import pallas as pl
from jax.experimental.pallas import tpu as pltpu
from jax.sharding import PartitionSpec as P

XN = 4
ZN = 8
CN = 2
GN = 4
H = 5
DH = 128
TOK = 128
PTOK = 64
ROWS = H * TOK
UNIT = 512
SPAN = 4096
SCALE = 1.0 / math.sqrt(DH)
C2 = SCALE * 1.4426950408889634
NEG = -1e30
MESH = pl.DeviceIdType.MESH
N_SEM = 112

COMP_AT = [1, 7, 2, 6, 3, 5, 4, 0]
PROMPT_AT = [0, 1, 7, 2, 6, 3, 5, 4]
PAIRS = [(1, 3), (0, 2)]
WIDE = 2 * ROWS


def token_slot(i):
    for p, pair in enumerate(PAIRS):
        if i in pair:
            return p, pair.index(i) * ROWS


def comp_slot(o):
    at = COMP_AT.index(o)
    return at // 2, (at % 2) * CN * TOK


def prompt_slot(o):
    at = PROMPT_AT.index(o)
    return 4 + at // 4, (at % 4) * CN * PTOK


def nt(a, b):
    return lax.dot_general(a, b, (((1,), (1,)), ((), ())), preferred_element_type=jnp.float32)


def nn(a, b):
    return lax.dot_general(a, b, (((1,), (0,)), ((), ())), preferred_element_type=jnp.float32)


def tn(a, b):
    return lax.dot_general(a, b, (((0,), (0,)), ((), ())), preferred_element_type=jnp.float32)


def kernel(
    owned,
    ids,
    pos,
    q_in,
    d_in,
    kv_in,
    p_in,
    dq_out,
    dc_out,
    dp_out,
    code,
    gq,
    gd,
    gqc,
    gkc,
    keys,
    wide,
    qs,
    ds,
    slots,
    mine,
    st,
    sbuf,
    norm,
    logit,
    second,
    acc,
    dqt,
    own_c,
    own_p,
    pair_s,
    pair_r,
    zs,
    zin_c,
    zin_p,
    via_c,
    via_c4,
    via_p,
    via_p4,
    dqs,
    dqr,
    yslots,
    send,
    recv,
    loc,
):
    f32, bf = jnp.float32, jnp.bfloat16
    s_at = lax.axis_index("seq")
    g = lax.axis_index("grp")
    x, z, c = s_at // (ZN * CN), lax.rem(s_at // CN, ZN), lax.rem(s_at, CN)

    def dev(dx, dz, dc, dg=0):
        xx, zz, gg = lax.rem(x + dx, XN), lax.rem(z + dz, ZN), lax.rem(g + dg, GN)
        cc = 1 - c if dc else c
        return (xx * (ZN * CN) + zz * CN + cc, gg)

    everyone = []
    count = [0]

    def start(src, dst, to):
        cp = pltpu.make_async_remote_copy(
            src_ref=src,
            dst_ref=dst,
            send_sem=send.at[count[0]],
            recv_sem=recv.at[count[0]],
            device_id=to,
            device_id_type=MESH,
        )
        count[0] += 1
        cp.start()
        everyone.append(cp)
        return cp

    def got(*cps):
        for cp in cps:
            cp.wait_recv()

    local_n = [0]

    def local(src, dst):
        cp = pltpu.make_async_copy(src, dst, loc.at[local_n[0]])
        local_n[0] += 1
        cp.start()
        return cp

    def comp_rows(o, other, lo=0, n=TOK):
        u, r = comp_slot(o)
        return keys.at[u, pl.ds(r + other * TOK + lo, n)]

    def prompt_rows(o, other, lo=0, n=PTOK):
        u, r = prompt_slot(o)
        return keys.at[u, pl.ds(r + other * PTOK + lo, n)]

    def code_row(o, other):
        u, r = comp_slot(o)
        return gkc.at[u * 4 + r // TOK + other]

    l_q = local(q_in, gq.at[0])
    l_d = local(d_in, gd.at[0])
    l_kv = local(kv_in, comp_rows(0, 0))
    l_p = local(p_in, slots.at[0])
    code[...] = jnp.broadcast_to(ids[...] * SPAN + pos[...], (8, TOK))
    gqc[0] = code[...]
    u0, r0 = comp_slot(0)
    gkc[u0 * 4 + r0 // TOK] = code[...]

    peer = dev(0, 0, 1)
    barrier = pltpu.get_barrier_semaphore()
    friends = [dev(i, 0, 0) for i in range(1, XN)] + [dev(0, 0, 0, i) for i in range(1, GN)]
    friends += [dev(0, i, 0) for i in range(1, ZN)] + [dev(0, i, 1) for i in range(ZN)]
    for to in friends:
        pl.semaphore_signal(barrier, inc=1, device_id=to, device_id_type=MESH)
    acc[...] = jnp.zeros_like(acc)
    dqt[...] = jnp.zeros_like(dqt)
    for p in range(2):
        st[p, 0:1, :] = jnp.full((1, WIDE), NEG, f32)
        st[p, 1:8, :] = jnp.zeros((7, WIDE), f32)
    for cp in (l_p, l_kv, l_q, l_d):
        cp.wait()
    pl.semaphore_wait(barrier, len(friends))

    y_cps = [start(slots.at[0], slots.at[GN - i], dev(0, 0, 0, i)) for i in range(1, GN)]
    code_cps = [start(code, code_row(0, 1), peer)]
    for i in range(1, ZN):
        code_cps.append(start(code, code_row(ZN - i, 0), dev(0, i, 0)))
        code_cps.append(start(code, code_row(ZN - i, 1), dev(0, i, 1)))
    for i in range(1, XN):
        code_cps.append(start(code, gqc.at[XN - i], dev(i, 0, 0)))
    k_cps, r_cps, p_cps, rp_cps, xq, xd = {}, {}, {}, {}, {}, {}
    mine_k = comp_rows(0, 0)
    xq[3] = start(gq.at[0], gq.at[3], dev(1, 0, 0))
    xd[1] = start(gd.at[0], gd.at[1], dev(3, 0, 0))
    for i in (1, 7):
        k_cps[8 - i] = start(mine_k, comp_rows(8 - i, 0), dev(0, i, 0))
    r_cps[0] = start(mine_k, comp_rows(0, 1), peer)
    for i in (2, 6):
        k_cps[8 - i] = start(mine_k, comp_rows(8 - i, 0), dev(0, i, 0))
    xd[3] = start(gd.at[0], gd.at[3], dev(1, 0, 0))
    xq[1] = start(gq.at[0], gq.at[1], dev(3, 0, 0))

    def relay(*os):
        for o in os:
            r_cps[o] = start(comp_rows(o, 0), comp_rows(o, 1), peer)

    def relay_p(*os):
        for o in os:
            rp_cps[o] = start(prompt_rows(o, 0), prompt_rows(o, 1), peer)

    def loop(n, body):
        def step(j, _):
            body(j)
            return 0

        lax.fori_loop(0, n, step, 0)

    def widen(j):
        wide[j // 4, pl.ds(pl.multiple_of(lax.rem(j, 4) * TOK, TOK), TOK), :] = jnp.broadcast_to(
            gkc[j, 0:1, :], (TOK, TOK)
        ).T

    def spread(i):
        p, at = token_slot(i)
        for h in range(H):
            rows = slice(at + h * TOK, at + (h + 1) * TOK)
            qs[p, rows, :] = gq[i, :, h * DH : (h + 1) * DH]
            ds[p, rows, :] = gd[i, :, h * DH : (h + 1) * DH]

    def visible(u, p, half):
        masks = []
        for i in PAIRS[p] if half is None else [PAIRS[p][half]]:
            qc = gqc[i, 0:1, :]
            kc = wide[u]
            base = qc - jnp.bitwise_and(qc, SPAN - 1)
            masks += [(kc <= qc) & (kc >= base)] * H
        return jnp.concatenate(masks, 1)

    def stat_tile(u, p, masked, half=None):
        at = slice(0, WIDE) if half is None else slice(half * ROWS, (half + 1) * ROWS)
        k = keys[u]
        s = nt(k[:, :DH], qs[p, at])
        if masked:
            s = jnp.where(visible(u, p, half), s, NEG)
        s = s * C2
        logit[u, p, :, at] = s
        dp = nt(k[:, DH:], ds[p, at])
        if not masked:
            second[u - 4, p] = dp
        m = st[p, 0:1, at]
        m2 = jnp.maximum(m, jnp.max(s, 0, keepdims=True))
        e = jnp.exp2(s - m2)
        a = jnp.exp2(m - m2)
        st[p, 0:1, at] = m2
        st[p, 1:2, at] = st[p, 1:2, at] * a + jnp.sum(e, 0, keepdims=True)
        st[p, 2:3, at] = st[p, 2:3, at] * a + jnp.sum(e * dp, 0, keepdims=True)

    spread(0)
    got(*y_cps)
    total = jnp.zeros((PTOK, 2 * DH), f32)
    for i in range(GN):
        w = (owned[lax.rem(g + i, GN)] == g).astype(f32)
        total = total + slots[i].astype(f32) * w
    mine[...] = total.astype(bf)
    for i in (1, 7, 2, 6):
        p_cps[8 - i] = start(mine, prompt_rows(8 - i, 0), dev(0, i, 0))
    rp_cps[0] = start(mine, prompt_rows(0, 1), peer)
    u, r = prompt_slot(0)
    keys[u, r : r + PTOK, :] = mine[...]
    got(k_cps[1], k_cps[7])
    relay(1, 7)
    got(*code_cps)
    loop(4 * 4, widen)
    half, phalf = TOK // 2, PTOK // 2
    got(k_cps[2], k_cps[6])
    k_cps[5] = start(comp_rows(6, 0), comp_rows(5, 0), dev(0, 1, 0))
    k_cps[3] = start(comp_rows(2, 0), comp_rows(3, 0), dev(0, 7, 0))
    far = [
        start(comp_rows(6, 0, 0, half), comp_rows(4, 0, 0, half), dev(0, 2, 0)),
        start(comp_rows(2, 0, half, half), comp_rows(4, 0, half, half), dev(0, 6, 0)),
    ]
    relay(2, 6)
    got(xq[3])
    xq[2] = start(gq.at[3], gq.at[2], dev(1, 0, 0))
    got(xd[1])
    xd[2] = start(gd.at[1], gd.at[2], dev(3, 0, 0))
    got(r_cps[1], r_cps[7])
    stat_tile(0, 1, True, 0)
    got(r_cps[2], r_cps[6])
    stat_tile(1, 1, True, 0)
    got(xd[3], xq[1])
    spread(1)
    spread(3)
    stat_tile(0, 0, True)
    got(p_cps[1], p_cps[7], p_cps[2], p_cps[6])
    p_cps[5] = start(prompt_rows(6, 0), prompt_rows(5, 0), dev(0, 1, 0))
    p_cps[3] = start(prompt_rows(2, 0), prompt_rows(3, 0), dev(0, 7, 0))
    pfar = [
        start(prompt_rows(6, 0, 0, phalf), prompt_rows(4, 0, 0, phalf), dev(0, 2, 0)),
        start(prompt_rows(2, 0, phalf, phalf), prompt_rows(4, 0, phalf, phalf), dev(0, 6, 0)),
    ]
    relay_p(1, 7, 2, 6)
    got(k_cps[3], k_cps[5], *far)
    relay(3, 5, 4)
    stat_tile(1, 0, True)
    got(r_cps[0], r_cps[3], r_cps[5], r_cps[4])
    loop(2, lambda u: stat_tile(2 + u, 0, True))
    got(xq[2], xd[2])
    spread(2)
    loop(2, lambda u: stat_tile(u, 1, True, 1))
    loop(2, lambda u: stat_tile(2 + u, 1, True))
    got(p_cps[3], p_cps[5], *pfar)
    relay_p(3, 5, 4)
    got(rp_cps[0], rp_cps[1], rp_cps[7], rp_cps[2])
    got(rp_cps[6], rp_cps[3], rp_cps[5], rp_cps[4])
    loop(2, lambda u: stat_tile(4 + u, 0, False))
    st_cps = []

    def share(i):
        p, at = token_slot(i)
        for j in range(1, XN):
            p2, at2 = token_slot((i - j) % XN)
            to = sbuf.at[XN - 1 - j, p2, :, pl.ds(at2, ROWS)]
            st_cps.append(start(st.at[p, :, pl.ds(at, ROWS)], to, dev(j, 0, 0)))

    share(1)
    share(3)
    loop(2, lambda u: stat_tile(4 + u, 1, False))
    share(0)
    share(2)
    got(*st_cps)
    for i in range(2):
        parts = [st[i]] + [sbuf[j, i] for j in range(XN - 1)]
        m = parts[0][0:1]
        for p in parts[1:]:
            m = jnp.maximum(m, p[0:1])
        l = jnp.zeros_like(m)
        w = jnp.zeros_like(m)
        for p in parts:
            a = jnp.exp2(p[0:1] - m)
            l = l + p[1:2] * a
            w = w + p[2:3] * a
        norm[i, 0:1, :] = m + jnp.log2(l)
        norm[i, 1:2, :] = w / l

    def grad_tile(e, u, i, lo=0, n=UNIT):
        kk = keys[u, lo : lo + n]
        qrow, drow = qs[i], ds[i]
        p = jnp.exp2(logit[u, i, lo : lo + n] - norm[i, 0:1, :])
        dp = second[u - 4, i] if u >= 4 else nt(kk[:, DH:], drow)
        dl = (p * (dp - norm[i, 1:2, :])).astype(bf)
        acc[e, :n, :DH] += nn(dl, qrow)
        acc[e, :n, DH:] += nn(p.astype(bf), drow)
        dqt[i] += tn(kk[:, :DH], dl)

    pair_cps, z_cps = {}, {}

    def emit(e, n, tiles):
        for t in range(tiles):
            r = (t * 2 + 1) * n
            pair_s[e, t * n : (t + 1) * n, :DH] = (acc[e, r : r + n, :DH] * SCALE).astype(bf)
            pair_s[e, t * n : (t + 1) * n, DH:] = acc[e, r : r + n, DH:].astype(bf)
        rows = pl.ds(0, n * tiles)
        pair_cps[e] = start(pair_s.at[e, rows], pair_r.at[e, rows], peer)

    v_cps = {}
    summed = set()

    def forward(e, n, tiles, own, zin, via, via4):
        if e not in summed:
            got(pair_cps[e])
            summed.add(e)
        half = n // 2
        for t, o in tiles:
            rows = slice(t * n, (t + 1) * n)
            mine_k = acc[e, t * 2 * n : (t * 2 + 1) * n, :DH] * SCALE
            mine_v = acc[e, t * 2 * n : (t * 2 + 1) * n, DH:]
            both = jnp.concatenate([mine_k, mine_v], 1) + pair_r[e, rows, :].astype(f32)
            if o == 0:
                own[...] = both
                continue
            if o in (2, 6):
                w = 0 if o == 2 else 1
                got(v_cps[(n, 3 + 2 * w)], v_cps[(n, 4, w)])
                extra = via4[w].astype(f32)
                none = jnp.zeros_like(extra)
                extra = jnp.concatenate([none, extra] if w else [extra, none], 0)
                both = both + via[w].astype(f32) + extra
            zs[e, rows, :] = both.astype(bf)
            src = zs.at[e, pl.ds(t * n, n)]
            if o == 3:
                v_cps[(n, 3)] = start(src, via.at[0], dev(0, 1, 0))
            elif o == 5:
                v_cps[(n, 5)] = start(src, via.at[1], dev(0, 7, 0))
            elif o == 4:
                v_cps[(n, 4, 0)] = start(zs.at[e, pl.ds(t * n, half)], via4.at[0], dev(0, 2, 0))
                v_cps[(n, 4, 1)] = start(zs.at[e, pl.ds(t * n + half, half)], via4.at[1], dev(0, 6, 0))
            else:
                z_cps[(e, o)] = start(src, zin.at[ZN - 1 - o], dev(0, o, 0))

    def forward_p(e, *tiles):
        forward(e, PTOK, tiles, own_p, zin_p, via_p, via_p4)

    def forward_c(e, *tiles):
        forward(e, TOK, tiles, own_c, zin_c, via_c, via_c4)

    dq_cps = []

    def put_query(i):
        p, at = token_slot(i)
        for h in range(H):
            part = dqt[p, :, at + h * TOK : at + (h + 1) * TOK].T * SCALE
            dqs[i, :, h * DH : (h + 1) * DH] = part.astype(bf)
        if i:
            dq_cps.append(start(dqs.at[i], dqr.at[XN - 1 - i], dev(i, 0, 0)))

    loop(2, lambda i: grad_tile(5, 5, i))
    emit(5, PTOK, 4)
    loop(2, lambda i: grad_tile(4, 4, i))
    emit(4, PTOK, 4)
    forward_p(5, (1, 3), (2, 5), (3, 4))
    loop(2, lambda i: grad_tile(3, 3, i, 0, UNIT // 2))
    emit(3, TOK, 1)
    forward_p(4, (0, 0), (1, 1), (2, 7))
    loop(2, lambda i: grad_tile(2, 2, i))
    emit(2, TOK, 2)
    forward_c(3, (0, 4))
    forward_p(4, (3, 2))
    forward_p(5, (0, 6))
    loop(2, lambda i: grad_tile(1, 1, i))
    emit(1, TOK, 2)
    forward_c(2, (0, 3), (1, 5))
    grad_tile(0, 0, 1)
    grad_tile(6, 3, 1, UNIT // 2, UNIT // 2)
    put_query(2)
    put_query(0)
    forward_c(1, (0, 2), (1, 6))
    got(*[cp for (e, o), cp in z_cps.items() if e in (4, 5)])
    total = own_p[...]
    for j in (0, 1, 5, 6):
        total = total + zin_p[j].astype(f32)
    yslots[0] = total.astype(bf)
    my_cps = [start(yslots.at[0], yslots.at[GN - j], dev(0, 0, 0, j)) for j in range(1, GN)]
    grad_tile(0, 0, 0)
    emit(0, TOK, 2)
    grad_tile(6, 3, 0, UNIT // 2, UNIT // 2)
    emit(6, TOK, 1)
    put_query(1)
    put_query(3)
    forward_c(0, (0, 1), (1, 7))
    forward_c(6, (0, 0))
    got(*my_cps)
    total = jnp.zeros((PTOK, 2 * DH), f32)
    wanted = owned[g]
    for i in range(GN):
        w = (wanted == lax.rem(g + i, GN)).astype(f32)
        total = total + yslots[i].astype(f32) * w
    dp_out[...] = total.astype(bf)
    got(*dq_cps)
    total = dqs[0].astype(f32)
    for j in range(XN - 1):
        total = total + dqr[j].astype(f32)
    dq_out[...] = total.astype(bf)
    got(*[cp for (e, o), cp in z_cps.items() if e not in (4, 5)])
    total = own_c[...]
    for j in (0, 1, 5, 6):
        total = total + zin_c[j].astype(f32)
    dc_out[...] = total.astype(bf)
    for cp in everyone:
        cp.wait_send()


def shards(queries, comp_kv, out_grad, comp_ids, comp_pos, prompt_kv, owned_prompt):
    bf, f32, i32 = jnp.bfloat16, jnp.float32, jnp.int32
    hbm = pl.BlockSpec(memory_space=pl.ANY)
    vmem = pl.BlockSpec(memory_space=pltpu.VMEM)
    smem = pl.BlockSpec(memory_space=pltpu.SMEM)
    grad_q, grad_c, grad_p = pl.pallas_call(
        kernel,
        out_shape=[
            jax.ShapeDtypeStruct((TOK, ROWS), bf),
            jax.ShapeDtypeStruct((TOK, 2 * DH), bf),
            jax.ShapeDtypeStruct((PTOK, 2 * DH), bf),
        ],
        in_specs=[smem, vmem, vmem] + [hbm] * 4,
        out_specs=[vmem] * 3,
        scratch_shapes=[
            pltpu.VMEM((8, TOK), i32),
            pltpu.VMEM((XN, TOK, ROWS), bf),
            pltpu.VMEM((XN, TOK, ROWS), bf),
            pltpu.VMEM((XN, 8, TOK), i32),
            pltpu.VMEM((16, 8, TOK), i32),
            pltpu.VMEM((6, UNIT, 2 * DH), bf),
            pltpu.VMEM((4, UNIT, TOK), i32),
            pltpu.VMEM((2, WIDE, DH), bf),
            pltpu.VMEM((2, WIDE, DH), bf),
            pltpu.VMEM((GN, PTOK, 2 * DH), bf),
            pltpu.VMEM((PTOK, 2 * DH), bf),
            pltpu.VMEM((2, 8, WIDE), f32),
            pltpu.VMEM((XN - 1, 2, 8, WIDE), f32),
            pltpu.VMEM((2, 8, WIDE), f32),
            pltpu.VMEM((6, 2, UNIT, WIDE), f32),
            pltpu.VMEM((2, 2, UNIT, WIDE), f32),
            pltpu.VMEM((7, UNIT, 2 * DH), f32),
            pltpu.VMEM((2, DH, WIDE), f32),
            pltpu.VMEM((TOK, 2 * DH), f32),
            pltpu.VMEM((PTOK, 2 * DH), f32),
            pltpu.VMEM((7, UNIT // 2, 2 * DH), bf),
            pltpu.VMEM((7, UNIT // 2, 2 * DH), bf),
            pltpu.VMEM((7, UNIT // 2, 2 * DH), bf),
            pltpu.VMEM((ZN - 1, TOK, 2 * DH), bf),
            pltpu.VMEM((ZN - 1, PTOK, 2 * DH), bf),
            pltpu.VMEM((2, TOK, 2 * DH), bf),
            pltpu.VMEM((2, TOK // 2, 2 * DH), bf),
            pltpu.VMEM((2, PTOK, 2 * DH), bf),
            pltpu.VMEM((2, PTOK // 2, 2 * DH), bf),
            pltpu.VMEM((XN, TOK, ROWS), bf),
            pltpu.VMEM((XN - 1, TOK, ROWS), bf),
            pltpu.VMEM((GN, PTOK, 2 * DH), bf),
            pltpu.SemaphoreType.DMA((N_SEM,)),
            pltpu.SemaphoreType.DMA((N_SEM,)),
            pltpu.SemaphoreType.DMA((4,)),
        ],
        compiler_params=pltpu.CompilerParams(
            collective_id=0, has_side_effects=True, vmem_limit_bytes=64 * 1024 * 1024
        ),
    )(owned_prompt, comp_ids, comp_pos, queries[0], out_grad[0], comp_kv[0], prompt_kv[0])
    return grad_q[None], grad_c[None], grad_p[None]


def solution(mesh):
    placed = (
        P("grp", "seq", None),
        P("grp", "seq", None),
        P("grp", "seq", None),
        P("grp", "seq"),
        P("grp", "seq"),
        P("grp", "seq", None),
        P(),
    )
    return jax.shard_map(
        shards,
        mesh=mesh,
        in_specs=placed,
        out_specs=(P("grp", "seq", None), P("grp", "seq", None), P("grp", "seq", None)),
        check_vma=False,
    )
```

profile of v0, /device:TPU:1, one launch (start us, length us, event | category | flops | bytes accessed | tf_op | source)
XLA Modules:
  0.0 69.7 jit_solution(6515900844589693563)
XLA Ops:
  0.6 66.0 %shard_map.94 = (bf16[128,640]{1,0:T(8,128)(2,1)}, bf16[128,256]{1,0:T(8,128)(2,1)}, bf16[64,256]{1,0:T(8,128)(2,1)}) custom-call(s32[4]{0:T(128)} %owned.1, s32[1,128]{1,0:T(1,128)} %ids.1, s32[1,128]{1,0:T(1,128)} %pos.1, bf16[128,640]{1,0:T(8,128)(2,1)} %bitcast.7, bf16[128,640]{1,0:T(8,128)(2,1)} %bitcast.8, bf16[128,256]{1,0:T(8,128)(2,1)} %bitcast.11, ...), custom_call_target="tpu_custom_call" | custom-call | tf_op jit(solution)/shard_map/pallas_call | solution.py:477
  66.7 0.0 copy-start
  66.7 1.6 %copy.13 = bf16[1,128,640]{2,1,0:T(8,128)(2,1)} copy(bf16[1,128,640]{2,1,0:T(8,128)(2,1)} %bitcast.9) | data formatting | bytes 327680
  68.3 0.0 copy-done
  68.3 0.0 copy-start.1
  68.3 0.6 copy.14
  68.9 0.1 copy-done.1
  69.1 0.6 copy.15
Async XLA Ops:
  66.7 1.6 %copy-start = (bf16[128,256]{1,0:T(8,128)(2,1)S(1)}, bf16[128,256]{1,0:T(8,128)(2,1)}, u32[]{:S(2)}) copy-start(bf16[128,256]{1,0:T(8,128)(2,1)} %get-tuple-element.7) | copy-start | bytes 196612
  68.3 0.8 %copy-start.1 = (bf16[64,256]{1,0:T(8,128)(2,1)S(1)}, bf16[64,256]{1,0:T(8,128)(2,1)}, u32[]{:S(2)}) copy-start(bf16[64,256]{1,0:T(8,128)(2,1)} %get-tuple-element.8) | copy-start | bytes 98308
where the time goes:
time: 70 us; the launch traced here: 69.7 us
  Pallas kernels  66 us (94%)
  local copies, waits for them, and re-layouts  3 us (4%)
    pallas_call x1, Pallas kernels, shards(): pl.pallas_call(kernel, out_shape=[jax.ShapeDtypeStruct((TOK, ROWS), bf),...  66 us
    unnamed x7, local copies, waits for them, and re-layouts  3 us

commit v1 on v0

--- a/solution.py
+++ b/solution.py
@@ -469,6 +469,11 @@
         cp.wait_send()
 
 
+def hand_over(*refs):
+    for i in range(3):
+        refs[3 + i][0] = refs[i][...]
+
+
 def shards(queries, comp_kv, out_grad, comp_ids, comp_pos, prompt_kv, owned_prompt):
     bf, f32, i32 = jnp.bfloat16, jnp.float32, jnp.int32
     hbm = pl.BlockSpec(memory_space=pl.ANY)
@@ -524,7 +529,14 @@
             collective_id=0, has_side_effects=True, vmem_limit_bytes=64 * 1024 * 1024
         ),
     )(owned_prompt, comp_ids, comp_pos, queries[0], out_grad[0], comp_kv[0], prompt_kv[0])
-    return grad_q[None], grad_c[None], grad_p[None]
+    results = (grad_q, grad_c, grad_p)
+    return pl.pallas_call(
+        hand_over,
+        out_shape=[jax.ShapeDtypeStruct((1,) + r.shape, r.dtype) for r in results],
+        in_specs=[vmem] * 3,
+        out_specs=[vmem] * 3,
+        compiler_params=pltpu.CompilerParams(vmem_limit_bytes=64 * 1024 * 1024),
+    )(*results)
 
 
 def solution(mesh):

time: 70 us -> 68.5 us (0.979)
  local copies, waits for them, and re-layouts: 3 us -> 0 us
  Pallas kernels: 66 us -> 67.7 us
    unnamed x7 -> x0, local copies, waits for them, and re-layouts: 3 us -> none
    pallas_call x0 -> x1, Pallas kernels: none -> 1.65 us  [shards(): pl.pallas_call(hand_over, out_shape=[jax.ShapeDtypeStruct((1,) + r.shape,...]
where the time goes in v1:
time: 68.5 us; the launch traced here: 68.3 us
  Pallas kernels  67.7 us (99%)
    pallas_call x1, Pallas kernels, shards(): pl.pallas_call(kernel, out_shape=[jax.ShapeDtypeStruct((TOK, ROWS), bf),...  66 us
    pallas_call x1, Pallas kernels, shards(): pl.pallas_call(hand_over, out_shape=[jax.ShapeDtypeStruct((1,) + r.shape,...  1.65 us

profile of v1, /device:TPU:1, one launch (start us, length us, event | category | flops | bytes accessed | tf_op | source)
XLA Modules:
  0.0 68.3 jit_solution(7209117305046445436)
XLA Ops:
  0.6 66.0 %shard_map.94 = (bf16[128,640]{1,0:T(8,128)(2,1)}, bf16[128,256]{1,0:T(8,128)(2,1)}, bf16[64,256]{1,0:T(8,128)(2,1)}) custom-call(s32[4]{0:T(128)} %owned.1, s32[1,128]{1,0:T(1,128)} %ids.1, s32[1,128]{1,0:T(1,128)} %pos.1, bf16[128,640]{1,0:T(8,128)(2,1)} %bitcast.4, bf16[128,640]{1,0:T(8,128)(2,1)} %bitcast.5, bf16[128,256]{1,0:T(8,128)(2,1)} %bitcast.6, ...), custom_call_target="tpu_custom_call" | custom-call | tf_op jit(solution)/shard_map/pallas_call | solution.py:482
  66.7 1.7 %shard_map.95 = (bf16[1,128,640]{2,1,0:T(8,128)(2,1)}, bf16[1,128,256]{2,1,0:T(8,128)(2,1)}, bf16[1,64,256]{2,1,0:T(8,128)(2,1)}) custom-call(bf16[128,640]{1,0:T(8,128)(2,1)} %get-tuple-element.6.refs_0_, bf16[128,256]{1,0:T(8,128)(2,1)} %get-tuple-element.7.refs_1_, bf16[64,256]{1,0:T(8,128)(2,1)} %get-tuple-element.8.refs_2_), custom_call_target="tpu_custom_call" | custom-call | tf_op jit(solution)/shard_map/pallas_call | solution.py:533

commit v2 on v1

--- a/solution.py
+++ b/solution.py
@@ -81,6 +81,7 @@
     slots,
     mine,
     st,
+    packed,
     sbuf,
     norm,
     logit,
@@ -315,30 +316,34 @@
     loop(2, lambda u: stat_tile(4 + u, 0, False))
     st_cps = []
 
-    def share(i):
-        p, at = token_slot(i)
+    def share(p):
+        packed[p, 0:4, :] = st[p, 0:4, :ROWS]
+        packed[p, 4:8, :] = st[p, 0:4, ROWS:]
         for j in range(1, XN):
-            p2, at2 = token_slot((i - j) % XN)
-            to = sbuf.at[XN - 1 - j, p2, :, pl.ds(at2, ROWS)]
-            st_cps.append(start(st.at[p, :, pl.ds(at, ROWS)], to, dev(j, 0, 0)))
-
+            p2 = token_slot((PAIRS[p][0] - j) % XN)[0]
+            st_cps.append(start(packed.at[p], sbuf.at[XN - 1 - j, p2], dev(j, 0, 0)))
+
+    def shared(k, p, row):
+        first = token_slot((PAIRS[p][0] + XN - 1 - k) % XN)[1] // ROWS
+        r0, r1 = 4 * first + row, 4 * (1 - first) + row
+        return jnp.concatenate([sbuf[k, p, r0 : r0 + 1, :], sbuf[k, p, r1 : r1 + 1, :]], 1)
+
+    share(0)
+    loop(2, lambda u: stat_tile(4 + u, 1, False))
     share(1)
-    share(3)
-    loop(2, lambda u: stat_tile(4 + u, 1, False))
-    share(0)
-    share(2)
     got(*st_cps)
     for i in range(2):
-        parts = [st[i]] + [sbuf[j, i] for j in range(XN - 1)]
-        m = parts[0][0:1]
+        parts = [[st[i, r : r + 1, :] for r in range(3)]]
+        parts += [[shared(j, i, r) for r in range(3)] for j in range(XN - 1)]
+        m = parts[0][0]
         for p in parts[1:]:
-            m = jnp.maximum(m, p[0:1])
+            m = jnp.maximum(m, p[0])
         l = jnp.zeros_like(m)
         w = jnp.zeros_like(m)
         for p in parts:
-            a = jnp.exp2(p[0:1] - m)
-            l = l + p[1:2] * a
-            w = w + p[2:3] * a
+            a = jnp.exp2(p[0] - m)
+            l = l + p[1] * a
+            w = w + p[2] * a
         norm[i, 0:1, :] = m + jnp.log2(l)
         norm[i, 1:2, :] = w / l
 
@@ -501,7 +506,8 @@
             pltpu.VMEM((GN, PTOK, 2 * DH), bf),
             pltpu.VMEM((PTOK, 2 * DH), bf),
             pltpu.VMEM((2, 8, WIDE), f32),
-            pltpu.VMEM((XN - 1, 2, 8, WIDE), f32),
+            pltpu.VMEM((2, 8, ROWS), f32),
+            pltpu.VMEM((XN - 1, 2, 8, ROWS), f32),
             pltpu.VMEM((2, 8, WIDE), f32),
             pltpu.VMEM((6, 2, UNIT, WIDE), f32),
             pltpu.VMEM((2, 2, UNIT, WIDE), f32),

time: 68.5 us -> 67.8 us (0.990)
  Pallas kernels: 67.7 us -> 66.9 us
    pallas_call x1, Pallas kernels: 66 us -> 65.3 us  [shards(): pl.pallas_call(kernel, out_shape=[jax.ShapeDtypeStruct((TOK, ROWS), bf),...]
where the time goes in v2:
time: 67.8 us; the launch traced here: 67.6 us
  Pallas kernels  66.9 us (99%)
    pallas_call x1, Pallas kernels, shards(): pl.pallas_call(kernel, out_shape=[jax.ShapeDtypeStruct((TOK, ROWS), bf),...  65.3 us
    pallas_call x1, Pallas kernels, shards(): pl.pallas_call(hand_over, out_shape=[jax.ShapeDtypeStruct((1,) + r.shape,...  1.65 us

profile of v2, /device:TPU:1, one launch (start us, length us, event | category | flops | bytes accessed | tf_op | source)
XLA Modules:
  0.0 67.6 jit_solution(1452876627222344770)
XLA Ops:
  0.6 65.3 %shard_map.94 = (bf16[128,640]{1,0:T(8,128)(2,1)}, bf16[128,256]{1,0:T(8,128)(2,1)}, bf16[64,256]{1,0:T(8,128)(2,1)}) custom-call(s32[4]{0:T(128)} %owned.1, s32[1,128]{1,0:T(1,128)} %ids.1, s32[1,128]{1,0:T(1,128)} %pos.1, bf16[128,640]{1,0:T(8,128)(2,1)} %bitcast.4, bf16[128,640]{1,0:T(8,128)(2,1)} %bitcast.5, bf16[128,256]{1,0:T(8,128)(2,1)} %bitcast.6, ...), custom_call_target="tpu_custom_call" | custom-call | tf_op jit(solution)/shard_map/pallas_call | solution.py:487
  65.9 1.7 %shard_map.95 = (bf16[1,128,640]{2,1,0:T(8,128)(2,1)}, bf16[1,128,256]{2,1,0:T(8,128)(2,1)}, bf16[1,64,256]{2,1,0:T(8,128)(2,1)}) custom-call(bf16[128,640]{1,0:T(8,128)(2,1)} %get-tuple-element.6.refs_0_, bf16[128,256]{1,0:T(8,128)(2,1)} %get-tuple-element.7.refs_1_, bf16[64,256]{1,0:T(8,128)(2,1)} %get-tuple-element.8.refs_2_), custom_call_target="tpu_custom_call" | custom-call | tf_op jit(solution)/shard_map/pallas_call | solution.py:539
